TPU v7x, 32 devices: a whole 2x2x4 slice. The times are simulated.
32 devices in a mesh: groups: 2 (over x), clu: 16 (over z, y, core).
Axes of the slice: x: 2, y: 2, z: 4, core: 2. Of those that a mesh axis runs over, the one named last changes fastest.
Arguments:
- charges: bfloat16 [64, 65536], P(None, ('groups', 'clu')), parts along dimension 1, may hold values from -6 to 6
- coords: bfloat16 [3, 65536], P(None, ('groups', 'clu')), parts along dimension 1, may hold values from -1 to 1
- requests: int32 [32, 16, 2], P(('groups', 'clu')), parts along dimension 0, may hold values from 0 to 7
- near_rows: int32 [32, 128], P(('groups', 'clu')), parts along dimension 0, may hold values from 0 to 7, as said below
- near_src: int32 [32, 128], P(('groups', 'clu')), parts along dimension 0, may hold values from 0 to 15, as said below
- local_pairs: int32 [32, 2, 16], P(('groups', 'clu')), parts along dimension 0, may hold values from 0 to 7, as said below
- far_rows: int32 [32, 256], P(('groups', 'clu')), parts along dimension 0, may hold values from 0 to 7, as said below
- far_slots: int32 [32, 256], P(('groups', 'clu')), parts along dimension 0, may hold values from 0 to 31
- far_left: bfloat16 [8192, 32, 256], P(('groups', 'clu')), parts along dimension 0, may hold values from -0.5 to 0.5
- far_right: bfloat16 [8192, 32, 256], P(('groups', 'clu')), parts along dimension 0, may hold values from -0.375 to 0.375
Outputs:
- potential: float32 [64, 65536], P(None, ('groups', 'clu')), parts along dimension 1
There are 2 independent parts, one for each index of `groups`. A program takes and returns all parts, laid end to end along the dimension named above; each array names one. Nothing has to cross between parts.
Inputs may be any that keep to these rules, and one draw needn't show every extreme that they name: requests[d, p, s] is the local index of a cluster of device p; device d reads that cluster into slot p * 2 + s. Within a device no pair (near_rows, near_src) repeats. near_src[d, k] = w names cluster 8 * (d + 1) + w, a cluster of one of the next two devices; indices past the last cluster mark unused pairs. local_pairs[d, 0, k] < local_pairs[d, 1, k], and no pair repeats within a device. Within a device no pair (far_rows, far_slots) repeats.
All inputs are finite; a program needn't handle non-finite values.
Results may differ from a plain program's by a relative error of at most 0.0029.
Values may be sent and summed in bfloat16 or wider, within the bound.
A program may use at most 128 MiB of HBM per device.

v0:
```python
import jax
import jax.numpy as jnp
from jax import lax
from jax.sharding import PartitionSpec as P

kernel_scale = 1.0 / 64.0
softening = 0.04


def from_behind(value, axis, steps):
    count = lax.axis_size(axis)
    leading, last = (max(0, -steps), min(count, count - steps))
    return lax.ppermute(value, axis, [(source, source + steps) for source in range(leading, last)])


def kernel_block(row_points, source_points):
    row_values = row_points.astype(jnp.float32)
    source_values = source_points.astype(jnp.float32)
    squared = (row_values[:, 0, :, None] - source_values[:, 0, None, :]) ** 2
    squared = squared + (row_values[:, 1, :, None] - source_values[:, 1, None, :]) ** 2
    squared = squared + (row_values[:, 2, :, None] - source_values[:, 2, None, :]) ** 2
    return (kernel_scale / jnp.sqrt(squared + softening)).astype(jnp.bfloat16)


def shards(
    charges,
    coords,
    requests,
    near_rows,
    near_src,
    local_pairs,
    far_rows,
    far_slots,
    far_left,
    far_right,
):
    columns, panel_count = charges.shape
    rank_count = far_left.shape[1]
    cl_size = far_left.shape[2]
    cluster_count = panel_count // cl_size
    slots_each = requests.shape[2]
    charge_blocks = charges.reshape(columns, cluster_count, cl_size).transpose(1, 0, 2)
    coord_blocks = coords.reshape(3, cluster_count, cl_size).transpose(1, 0, 2)
    labels = jnp.arange(cluster_count, dtype=jnp.int32)

    def spread(cluster_ids, dtype):
        return (cluster_ids[:, None] == labels[None, :]).astype(dtype)

    def add_rows(potential, cluster_ids, values):
        return potential + jnp.einsum(
            "pr,pna->rna", spread(cluster_ids, jnp.float32), values, precision=lax.Precision.HIGHEST
        )

    def local_step(potential, pair_ids):
        firsts = pair_ids[0]
        seconds = pair_ids[1]
        kernel = kernel_block(coord_blocks[firsts], coord_blocks[seconds])
        forward = jnp.einsum(
            "pab,pnb->pna", kernel, charge_blocks[seconds], preferred_element_type=jnp.float32
        )
        reverse = jnp.einsum(
            "pab,pna->pnb", kernel, charge_blocks[firsts], preferred_element_type=jnp.float32
        )
        potential = add_rows(potential, firsts, forward)
        potential = add_rows(potential, seconds, reverse)
        return (potential, None)

    potential = jnp.zeros((cluster_count, columns, cl_size), jnp.float32)
    pair_table = local_pairs.reshape(2, -1, 8).transpose(1, 0, 2)
    potential, _ = lax.scan(local_step, potential, pair_table)
    fetched_near = []
    for step in (1, 2):
        fetched_near.append(from_behind((charge_blocks, coord_blocks), "clu", -step))
    window_charge = jnp.concatenate([fetched_near[0][0], fetched_near[1][0]], axis=0)
    window_coord = jnp.concatenate([fetched_near[0][1], fetched_near[1][1]], axis=0)
    every_charge, every_coord = (
        lax.all_gather(charge_blocks, "clu", axis=0, tiled=True),
        lax.all_gather(coord_blocks, "clu", axis=0, tiled=True),
    )
    slot_total = requests.shape[1] * slots_each
    sources = jnp.arange(
        slot_total, dtype=jnp.int32
    ) // slots_each * cluster_count + requests.reshape(-1)
    fetched_charge = every_charge[sources]

    def near_step(potential, inputs):
        rows_here, window_here = inputs
        kernel = kernel_block(coord_blocks[rows_here], window_coord[window_here])
        forward = jnp.einsum(
            "pab,pnb->pna", kernel, window_charge[window_here], preferred_element_type=jnp.float32
        )
        reverse = jnp.einsum(
            "pab,pna->pnb", kernel, charge_blocks[rows_here], preferred_element_type=jnp.float32
        )
        potential = add_rows(potential, rows_here, forward)
        return (potential, reverse)

    near_inputs = (near_rows[0].reshape(-1, 16), near_src[0].reshape(-1, 16))
    potential, returned_blocks = lax.scan(near_step, potential, near_inputs)
    outgoing = returned_blocks.reshape(-1, columns, cl_size)
    source_marks = near_src[0].astype(jnp.float32)
    for step in (1, 2):
        got, marks = (
            from_behind(outgoing.astype(jnp.bfloat16), "clu", step).astype(outgoing.dtype),
            from_behind(source_marks.astype(jnp.bfloat16), "clu", step).astype(source_marks.dtype),
        )
        wanted_marks = (labels + (step - 1) * cluster_count).astype(jnp.float32)
        match = (marks[:, None] == wanted_marks[None, :]).astype(jnp.float32)
        potential = potential + jnp.einsum(
            "pr,pna->rna", match, got, precision=lax.Precision.HIGHEST
        )

    def far_step(potential, inputs):
        rows_here, slots_here, left_here, right_here = inputs
        source_charge = fetched_charge[slots_here]
        coefficients = jnp.einsum(
            "pnb,pkb->pnk", source_charge, right_here, preferred_element_type=jnp.float32
        ).astype(jnp.bfloat16)
        far_term = jnp.einsum(
            "pnk,pka->pna", coefficients, left_here, preferred_element_type=jnp.float32
        )
        return (add_rows(potential, rows_here, far_term), None)

    far_inputs = (
        far_rows[0].reshape(-1, 64),
        far_slots[0].reshape(-1, 64),
        far_left.reshape(-1, 64, rank_count, cl_size),
        far_right.reshape(-1, 64, rank_count, cl_size),
    )
    potential, _ = lax.scan(far_step, potential, far_inputs)
    return potential.transpose(1, 0, 2).reshape(columns, panel_count)


def solution(mesh):
    in_specs = (
        P(None, ("groups", "clu")),
        P(None, ("groups", "clu")),
        P(("groups", "clu"), None, None),
        P(("groups", "clu"), None),
        P(("groups", "clu"), None),
        P(("groups", "clu"), None, None),
        P(("groups", "clu"), None),
        P(("groups", "clu"), None),
        P(("groups", "clu"), None, None),
        P(("groups", "clu"), None, None),
    )
    out_specs = P(None, ("groups", "clu"))
    return jax.shard_map(shards, mesh=mesh, in_specs=in_specs, out_specs=out_specs, check_vma=False)
```

profile of v0, /device:TPU:19, one launch (start us, length us, event | category | flops | bytes accessed | tf_op | source)
XLA Modules:
  0.0 345.2 jit_solution(7445266443116022571)
XLA Ops:
  19.9 19.5 %while.38 = (s32[]{:T(128)}, f32[8,64,256]{2,0,1:T(8,128)S(1)}, s32[2,2,8]{2,0,1:T(2,128)S(1)}, bf16[8,64,256]{2,1,0:T(8,128)(2,1)}, bf16[8,3,256]{2,1,0:T(4,128)(2,1)}, /*index=5*/s32[]{:T(128)}, s32[]{:T(128)}) while((s32[]{:T(128)}, f32[8,64,256]{2,0,1:T(8,128)S(1)}, s32[2,2,8]{2,0,1:T(2,128)S(1)}, ...), condition=%wide.region_1.2_spmd.clone.clone, body=%wide.region_0.1_spmd.clone.clone.sunk | while | flops 171313328 | bytes 7168767 | solution.py:70
  41.5 89.3 %while.36 = (s32[]{:T(128)}, f32[8,64,256]{2,0,1:T(8,128)S(1)}, bf16[8,16,64,256]{3,2,1,0:T(8,128)(2,1)}, s32[8,16]{1,0:T(8,128)S(1)}, s32[8,16]{1,0:T(8,128)S(1...) while((s32[]{:T(128)}, f32[8,64,256]{2,0,1:T(8,128)S(1)}, ...), condition=%wide.region_3.4_spmd.clone, body=%wide.region_2.3_spmd.clone.sunk | while | flops 316803296 | bytes 9085909 | solution.py:99
  44.2 3.4 fusion.119
  55.4 3.4 fusion.119
  66.6 3.4 fusion.119
  77.7 3.4 fusion.119
  83.0 3.3 fusion.121
  88.9 3.4 fusion.119
  100.1 3.4 fusion.119
  111.2 3.4 fusion.119
  122.4 3.4 fusion.119
  130.9 6.6 %copy.37 = bf16[8,16,64,256]{3,1,0,2:T(8,128)(2,1)} copy(bf16[8,16,64,256]{3,2,1,0:T(8,128)(2,1)} %get-tuple-element.137) | data formatting | bytes 8388608 | tf_op jit(solution)/shard_map/convert_element_type | solution.py:104
  140.3 4.0 %collective-permute-start.7 = (bf16[128,64,256]{2,0,1:T(8,128)(2,1)}, bf16[128,64,256]{2,0,1:T(8,128)(2,1)}, u32[]{:S(2)}, u32[]{:S(2)}) collective-permute-start(bf16[128,64,256]{2,0,1:T(8,128)(2,1)} %bitcast.7), channel_id=1, source_target_pairs={{0,2},{1,3},{2,4},{3,5},{4,6},{5,7},{6,8},{7,9},{8,10},{9,11},{10,... | collective-permute-start | bytes 12582920 | tf_op jit(solution)/shard_map/ppermute | solution.py:13
  150.7 125.2 %collective-permute-done.4 = bf16[128]{0:T(256)(128)(2,1)S(1)} collective-permute-done((bf16[128]{0:T(256)(128)(2,1)S(1)}, bf16[128]{0:T(256)(128)(2,1)S(1)}, u32[]{:S(2)}, u32[]{:S(2)}) %collective-permute-start.4) | collective-permute-done | bytes 288 | tf_op jit(solution)/shard_map/ppermute | solution.py:13
  281.3 3.7 %add_add_fusion = f32[8,64,256]{2,0,1:T(8,128)} fusion(f32[8,64,256]{2,0,1:T(8,128)S(1)} %get-tuple-element.136, f32[8,64,256]{2,0,1:T(8,128)S(1)} %fusion.60, bf16[128,64,256]{2,0,1:T(8,128)(2,1)} %collective-permute-done.7, f32[128]{0:T(128)S(1)} %convert_element_type.74, f32[8]{0:T(128)S(1)} %add_convert_fusion), kind=kOutput, calls=%fused_computation.95 | convolution fusion | flops 33817600 | bytes 5767712 | tf_op jit(solution)/shard_map/pr,pna->rna/dot_general | solution.py:109
  287.8 48.6 %while.37 = (s32[]{:T(128)}, f32[8,64,256]{2,0,1:T(8,128)}, s32[4,64]{1,0:T(4,128)S(1)}, s32[4,64]{1,0:T(4,128)S(1)}, bf16[32,64,256]{2,1,0:T(8,128)(2,1)S(1)}, ...) while((s32[]{:T(128)}, f32[8,64,256]{2,0,1:T(8,128)}, ...), condition=%wide.region_5.6_spmd.clone, body=%wide.region_4.5_spmd.clone.sunk | while | flops 235144896 | bytes 17832804 | solution.py:130
  288.5 4.7 %fusion.128 = f32[64,64,256]{2,1,0:T(8,128)} fusion(bf16[64,64,256]{2,1,0:T(8,128)(2,1)S(1)} %gather_fusion.4, bf16[4,64,32,256]{3,2,1,0:T(8,128)(2,1)} %get-tuple-element.562, s32[]{:T(128)S(6)} %copy.139, bf16[4,64,32,256]{3,2,1,0:T(8,128)(2,1)} %get-tuple-element.561), kind=kOutput, calls=%fused_computation.45.clone.1 | convolution fusion | flops 134348800 | bytes 8389632 | tf_op jit(solution)/shard_map/while/body/eval_jaxpr/pnk,pka->pna/dot_general | solution.py:119
  293.3 6.7 %fusion.130 = f32[8,64,256]{2,0,1:T(8,128)} fusion(f32[8,64,256]{2,0,1:T(8,128)} %get-tuple-element.549, f32[64,64,256]{2,1,0:T(8,128)} %fusion.128, s32[64]{0:T(128)S(1)} %fusion.129), kind=kOutput, calls=%fused_computation.46.clone.1 | convolution fusion | flops 100794880 | bytes 5243136 | tf_op jit(solution)/shard_map/while/body/eval_jaxpr/pr,pna->rna/dot_general | solution.py:50
  300.7 4.7 %fusion.128 = f32[64,64,256]{2,1,0:T(8,128)} fusion(bf16[64,64,256]{2,1,0:T(8,128)(2,1)S(1)} %gather_fusion.4, bf16[4,64,32,256]{3,2,1,0:T(8,128)(2,1)} %get-tuple-element.562, s32[]{:T(128)S(6)} %copy.139, bf16[4,64,32,256]{3,2,1,0:T(8,128)(2,1)} %get-tuple-element.561), kind=kOutput, calls=%fused_computation.45.clone.1 | convolution fusion | flops 134348800 | bytes 8389632 | tf_op jit(solution)/shard_map/while/body/eval_jaxpr/pnk,pka->pna/dot_general | solution.py:119
  305.4 6.7 %fusion.130 = f32[8,64,256]{2,0,1:T(8,128)} fusion(f32[8,64,256]{2,0,1:T(8,128)} %get-tuple-element.549, f32[64,64,256]{2,1,0:T(8,128)} %fusion.128, s32[64]{0:T(128)S(1)} %fusion.129), kind=kOutput, calls=%fused_computation.46.clone.1 | convolution fusion | flops 100794880 | bytes 5243136 | tf_op jit(solution)/shard_map/while/body/eval_jaxpr/pr,pna->rna/dot_general | solution.py:50
  312.8 4.7 %fusion.128 = f32[64,64,256]{2,1,0:T(8,128)} fusion(bf16[64,64,256]{2,1,0:T(8,128)(2,1)S(1)} %gather_fusion.4, bf16[4,64,32,256]{3,2,1,0:T(8,128)(2,1)} %get-tuple-element.562, s32[]{:T(128)S(6)} %copy.139, bf16[4,64,32,256]{3,2,1,0:T(8,128)(2,1)} %get-tuple-element.561), kind=kOutput, calls=%fused_computation.45.clone.1 | convolution fusion | flops 134348800 | bytes 8389632 | tf_op jit(solution)/shard_map/while/body/eval_jaxpr/pnk,pka->pna/dot_general | solution.py:119
  317.5 6.7 %fusion.130 = f32[8,64,256]{2,0,1:T(8,128)} fusion(f32[8,64,256]{2,0,1:T(8,128)} %get-tuple-element.549, f32[64,64,256]{2,1,0:T(8,128)} %fusion.128, s32[64]{0:T(128)S(1)} %fusion.129), kind=kOutput, calls=%fused_computation.46.clone.1 | convolution fusion | flops 100794880 | bytes 5243136 | tf_op jit(solution)/shard_map/while/body/eval_jaxpr/pr,pna->rna/dot_general | solution.py:50
  324.9 4.7 %fusion.128 = f32[64,64,256]{2,1,0:T(8,128)} fusion(bf16[64,64,256]{2,1,0:T(8,128)(2,1)S(1)} %gather_fusion.4, bf16[4,64,32,256]{3,2,1,0:T(8,128)(2,1)} %get-tuple-element.562, s32[]{:T(128)S(6)} %copy.139, bf16[4,64,32,256]{3,2,1,0:T(8,128)(2,1)} %get-tuple-element.561), kind=kOutput, calls=%fused_computation.45.clone.1 | convolution fusion | flops 134348800 | bytes 8389632 | tf_op jit(solution)/shard_map/while/body/eval_jaxpr/pnk,pka->pna/dot_general | solution.py:119
  329.7 6.7 %fusion.130 = f32[8,64,256]{2,0,1:T(8,128)} fusion(f32[8,64,256]{2,0,1:T(8,128)} %get-tuple-element.549, f32[64,64,256]{2,1,0:T(8,128)} %fusion.128, s32[64]{0:T(128)S(1)} %fusion.129), kind=kOutput, calls=%fused_computation.46.clone.1 | convolution fusion | flops 100794880 | bytes 5243136 | tf_op jit(solution)/shard_map/while/body/eval_jaxpr/pr,pna->rna/dot_general | solution.py:50
  (274 shorter events, 114.3 us)
Async XLA Ops:
  6.5 278.4 %all-gather.2.cloned.1.call-start = ((), (), s32[]{:S(2)}) async-start(), calls=%async_computation | async-start | bytes 4456448 | tf_op jit(solution)/shard_map/all_gather | solution.py:77
  7.5 33.8 %collective-permute-start.1 = (bf16[8,64,256]{2,0,1:T(8,128)(2,1)S(1)}, bf16[8,64,256]{2,0,1:T(8,128)(2,1)S(1)}, u32[]{:S(2)}, u32[]{:S(2)}) collective-permute-start(bf16[8,64,256]{2,0,1:T(8,128)(2,1)S(1)} %bitcast.203), channel_id=1, source_target_pairs={{2,0},{3,1},{4,2},{5,3},{6,4},{7,5},{8,6},{9,7},{10,8},{11,9},{12,... | collective-permute-start | bytes 786440 | tf_op jit(solution)/shard_map/ppermute | solution.py:13
  10.6 30.7 %collective-permute-start = (bf16[8,64,256]{2,0,1:T(8,128)(2,1)S(1)}, bf16[8,64,256]{2,0,1:T(8,128)(2,1)S(1)}, u32[]{:S(2)}, u32[]{:S(2)}) collective-permute-start(bf16[8,64,256]{2,0,1:T(8,128)(2,1)S(1)} %bitcast.204), channel_id=1, source_target_pairs={{1,0},{2,1},{3,2},{4,3},{5,4},{6,5},{7,6},{8,7},{9,8},{10,9},{11,1... | collective-permute-start | bytes 786440 | tf_op jit(solution)/shard_map/ppermute | solution.py:13
  13.5 27.8 %collective-permute-start.3 = (bf16[8,3,256]{2,1,0:T(4,128)(2,1)}, bf16[8,3,256]{2,1,0:T(4,128)(2,1)S(1)}, u32[]{:S(2)}, u32[]{:S(2)}) collective-permute-start(bf16[8,3,256]{2,1,0:T(4,128)(2,1)} %bitcast.200), channel_id=1, source_target_pairs={{2,0},{3,1},{4,2},{5,3},{6,4},{7,5},{8,6},{9,7},{10,8},{11,9},{12,... | collective-permute-start | bytes 36872 | tf_op jit(solution)/shard_map/ppermute | solution.py:13
  15.6 25.7 %collective-permute-start.2 = (bf16[8,3,256]{2,1,0:T(4,128)(2,1)}, bf16[8,3,256]{2,1,0:T(4,128)(2,1)S(1)}, u32[]{:S(2)}, u32[]{:S(2)}) collective-permute-start(bf16[8,3,256]{2,1,0:T(4,128)(2,1)} %bitcast.201), channel_id=1, source_target_pairs={{1,0},{2,1},{3,2},{4,3},{5,4},{6,5},{7,6},{8,7},{9,8},{10,9},{11,1... | collective-permute-start | bytes 36872 | tf_op jit(solution)/shard_map/ppermute | solution.py:13
  19.9 20.0 %copy-start.5 = (s32[1,128]{1,0:T(1,128)S(1)}, s32[1,128]{1,0:T(1,128)}, u32[]{:S(2)}) copy-start(s32[1,128]{1,0:T(1,128)} %param.20) | copy-start | bytes 1540
  19.9 20.6 %copy-start.6 = (s32[1,128]{1,0:T(1,128)S(1)}, s32[1,128]{1,0:T(1,128)}, u32[]{:S(2)}) copy-start(s32[1,128]{1,0:T(1,128)} %param.19) | copy-start | bytes 1540
  19.9 6.7 %copy-start = (bf16[8,64,256]{2,1,0:T(8,128)(2,1)S(1)}, bf16[8,64,256]{2,1,0:T(8,128)(2,1)}, u32[]{:S(2)}) copy-start(bf16[8,64,256]{2,1,0:T(8,128)(2,1)} %get-tuple-element.506) | copy-start | bytes 786436 | tf_op jit(solution)/shard_map/while
  29.7 6.7 %copy-start = (bf16[8,64,256]{2,1,0:T(8,128)(2,1)S(1)}, bf16[8,64,256]{2,1,0:T(8,128)(2,1)}, u32[]{:S(2)}) copy-start(bf16[8,64,256]{2,1,0:T(8,128)(2,1)} %get-tuple-element.506) | copy-start | bytes 786436 | tf_op jit(solution)/shard_map/while
  44.2 4.7 %copy-start.1 = (bf16[8,64,256]{2,1,0:T(8,128)(2,1)S(1)}, bf16[8,64,256]{2,1,0:T(8,128)(2,1)}, u32[]{:S(2)}) copy-start(bf16[8,64,256]{2,1,0:T(8,128)(2,1)} %get-tuple-element.538) | copy-start | bytes 786436 | tf_op jit(solution)/shard_map/while
  55.4 4.7 %copy-start.1 = (bf16[8,64,256]{2,1,0:T(8,128)(2,1)S(1)}, bf16[8,64,256]{2,1,0:T(8,128)(2,1)}, u32[]{:S(2)}) copy-start(bf16[8,64,256]{2,1,0:T(8,128)(2,1)} %get-tuple-element.538) | copy-start | bytes 786436 | tf_op jit(solution)/shard_map/while
  66.6 4.7 %copy-start.1 = (bf16[8,64,256]{2,1,0:T(8,128)(2,1)S(1)}, bf16[8,64,256]{2,1,0:T(8,128)(2,1)}, u32[]{:S(2)}) copy-start(bf16[8,64,256]{2,1,0:T(8,128)(2,1)} %get-tuple-element.538) | copy-start | bytes 786436 | tf_op jit(solution)/shard_map/while
  77.7 4.7 %copy-start.1 = (bf16[8,64,256]{2,1,0:T(8,128)(2,1)S(1)}, bf16[8,64,256]{2,1,0:T(8,128)(2,1)}, u32[]{:S(2)}) copy-start(bf16[8,64,256]{2,1,0:T(8,128)(2,1)} %get-tuple-element.538) | copy-start | bytes 786436 | tf_op jit(solution)/shard_map/while
  88.9 4.7 %copy-start.1 = (bf16[8,64,256]{2,1,0:T(8,128)(2,1)S(1)}, bf16[8,64,256]{2,1,0:T(8,128)(2,1)}, u32[]{:S(2)}) copy-start(bf16[8,64,256]{2,1,0:T(8,128)(2,1)} %get-tuple-element.538) | copy-start | bytes 786436 | tf_op jit(solution)/shard_map/while
  100.1 4.7 %copy-start.1 = (bf16[8,64,256]{2,1,0:T(8,128)(2,1)S(1)}, bf16[8,64,256]{2,1,0:T(8,128)(2,1)}, u32[]{:S(2)}) copy-start(bf16[8,64,256]{2,1,0:T(8,128)(2,1)} %get-tuple-element.538) | copy-start | bytes 786436 | tf_op jit(solution)/shard_map/while
  111.2 4.7 %copy-start.1 = (bf16[8,64,256]{2,1,0:T(8,128)(2,1)S(1)}, bf16[8,64,256]{2,1,0:T(8,128)(2,1)}, u32[]{:S(2)}) copy-start(bf16[8,64,256]{2,1,0:T(8,128)(2,1)} %get-tuple-element.538) | copy-start | bytes 786436 | tf_op jit(solution)/shard_map/while
  122.4 4.7 %copy-start.1 = (bf16[8,64,256]{2,1,0:T(8,128)(2,1)S(1)}, bf16[8,64,256]{2,1,0:T(8,128)(2,1)}, u32[]{:S(2)}) copy-start(bf16[8,64,256]{2,1,0:T(8,128)(2,1)} %get-tuple-element.538) | copy-start | bytes 786436 | tf_op jit(solution)/shard_map/while
  130.9 18.3 %copy-start.2 = (s32[1,16,2]{1,2,0:T(2,128)S(1)}, s32[1,16,2]{1,2,0:T(2,128)}, u32[]{:S(2)}) copy-start(s32[1,16,2]{1,2,0:T(2,128)} %param.18) | copy-start | bytes 388
  130.9 18.5 %copy-start.3 = (s32[1,256]{1,0:T(1,128)S(1)}, s32[1,256]{1,0:T(1,128)}, u32[]{:S(2)}) copy-start(s32[1,256]{1,0:T(1,128)} %param.22) | copy-start | bytes 3076
  130.9 19.2 %copy-start.4 = (s32[1,256]{1,0:T(1,128)S(1)}, s32[1,256]{1,0:T(1,128)}, u32[]{:S(2)}) copy-start(s32[1,256]{1,0:T(1,128)} %param.23) | copy-start | bytes 3076
  137.5 140.9 %collective-permute-start.5 = (bf16[128,64,256]{2,0,1:T(8,128)(2,1)}, bf16[128,64,256]{2,0,1:T(8,128)(2,1)}, u32[]{:S(2)}, u32[]{:S(2)}) collective-permute-start(bf16[128,64,256]{2,0,1:T(8,128)(2,1)} %bitcast.7), channel_id=1, source_target_pairs={{0,1},{1,2},{2,3},{3,4},{4,5},{5,6},{6,7},{7,8},{8,9},{9,10},{10,1... | collective-permute-start | bytes 12582920 | tf_op jit(solution)/shard_map/ppermute | solution.py:13
  140.3 141.0 %collective-permute-start.7 = (bf16[128,64,256]{2,0,1:T(8,128)(2,1)}, bf16[128,64,256]{2,0,1:T(8,128)(2,1)}, u32[]{:S(2)}, u32[]{:S(2)}) collective-permute-start(bf16[128,64,256]{2,0,1:T(8,128)(2,1)} %bitcast.7), channel_id=1, source_target_pairs={{0,2},{1,3},{2,4},{3,5},{4,6},{5,7},{6,8},{7,9},{8,10},{9,11},{10,... | collective-permute-start | bytes 12582920 | tf_op jit(solution)/shard_map/ppermute | solution.py:13
  144.3 131.6 %collective-permute-start.4 = (bf16[128]{0:T(256)(128)(2,1)S(1)}, bf16[128]{0:T(256)(128)(2,1)S(1)}, u32[]{:S(2)}, u32[]{:S(2)}) collective-permute-start(bf16[128]{0:T(256)(128)(2,1)S(1)} %get-tuple-element.318), channel_id=1, source_target_pairs={{0,1},{1,2},{2,3},{3,4},{4,5},{5,6},{6,7},{7,8},{8,9},{9,10},{10,1... | collective-permute-start | bytes 776 | tf_op jit(solution)/shard_map/ppermute | solution.py:13
  146.5 131.8 %collective-permute-start.6 = (bf16[128]{0:T(256)(128)(2,1)S(1)}, bf16[128]{0:T(256)(128)(2,1)S(1)}, u32[]{:S(2)}, u32[]{:S(2)}) collective-permute-start(bf16[128]{0:T(256)(128)(2,1)S(1)} %get-tuple-element.318), channel_id=1, source_target_pairs={{0,2},{1,3},{2,4},{3,5},{4,6},{5,7},{6,8},{7,9},{8,10},{9,11},{10,... | collective-permute-start | bytes 776 | tf_op jit(solution)/shard_map/ppermute | solution.py:13
Sparse Core Ops, SparseCore 0:
  19.3 50.6 all-gather.1
where the time goes:
time: 347 us; the launch traced here: 345 us
  waiting for transfers between devices  128 us (37%)
  matrix products  125 us (36%)
  local copies, waits for them, and re-layouts  52.8 us (15%)
  starting transfers between devices  22.4 us (6%)
  between operations  13.6 us (4%)
    ppermute x8, waiting for transfers between devices, from_behind(): lax.ppermute(value, axis, [(source, source + steps) for source in range(l...  128 us
    dot_general x16, matrix products, add_rows(): jnp.einsum('pr,pna->rna', spread(cluster_ids, jnp.float32), values, preci...  38.9 us
    dot_general x8, matrix products, near_step(): jnp.einsum('pab,pnb->pna', kernel, window_charge[window_here], preferred_...  27.4 us
    dot_general x8, matrix products, near_step(): jnp.einsum('pab,pna->pnb', kernel, charge_blocks[rows_here], preferred_el...  25.9 us
    ppermute x8, starting transfers between devices, from_behind(): lax.ppermute(value, axis, [(source, source + steps) for source in range(l...  22.4 us
    dot_general x4, matrix products, far_step(): jnp.einsum('pnk,pka->pna', coefficients, left_here, preferred_element_typ...  18.9 us
    gather x16, local copies, waits for them, and re-layouts, near_step(): kernel = kernel_block(coord_blocks[rows_here], window_coord[window_here])  15.2 us
  transfers between devices with their start and end apart: 9, of which 2 were waited for; matrix products, arithmetic and copies ran while one was open for 36% of the time, Pallas kernels for 0%

commit v1 on v0

v1 whole, which is shorter than its diff:
```python
import functools

import jax
import jax.numpy as jnp
from jax import lax
from jax.experimental import pallas as pl
from jax.experimental.pallas import tpu as pltpu
from jax.sharding import PartitionSpec as P

kernel_scale = 1.0 / 64.0
softening = 0.04
MESH = pl.DeviceIdType.MESH
FEATURES = 16
WINDOW = (-2, -1, 1, 2)


def split3(values):
    high = values.astype(jnp.bfloat16)
    rest = values - high.astype(jnp.float32)
    mid = rest.astype(jnp.bfloat16)
    low = (rest - mid.astype(jnp.float32)).astype(jnp.bfloat16)
    return high.astype(jnp.float32), mid.astype(jnp.float32), low.astype(jnp.float32)


def point_features(coords):
    wide = coords.astype(jnp.float32)
    factor = 1.0 / (kernel_scale * kernel_scale)
    norm = (jnp.sum(wide * wide, axis=0, keepdims=True) + 0.5 * softening) * factor
    norms = jnp.concatenate(split3(norm), axis=0)
    ones = jnp.ones_like(norms)
    zeros = jnp.zeros((FEATURES - 9, wide.shape[1]), jnp.float32)
    source = jnp.concatenate([wide, norms, ones, zeros], axis=0)
    target = jnp.concatenate([wide * (-2.0 * factor), ones, norms, zeros], axis=0)
    return source, target


def body(
    n, dense,
    inv_ref, req_ref, q_ref, x_ref, mask_ref, left_hbm, right_hbm,
    out_ref,
    qbuf, fown, fbuf, ft, gown, qgroup, left_v, right_v,
    send_sem, recv_sem, fsend_sem, frecv_sem, load_sem,
):
    columns, width = q_ref.shape
    size = left_hbm.shape[2]
    rank = left_hbm.shape[1]
    clusters = width // size
    zs = n // 4
    me = lax.axis_index("clu")
    z = me // 4
    y = (me // 2) % 2
    core = me % 2
    sib = me + 1 - 2 * core
    other_y = me + 2 - 4 * y

    def block_id(z_at, y_at, core_at):
        return z_at * 4 + y_at * 2 + core_at

    barrier = pltpu.get_barrier_semaphore()
    partners = [(z > 0, me - 4), (z < zs - 1, me + 4), (None, other_y), (None, sib)]
    partners += [((me + off >= 0) & (me + off < n), me + off) for off in WINDOW]
    for valid, partner in partners:
        def greet(partner=partner):
            pl.semaphore_signal(barrier, inc=1, device_id={"clu": partner}, device_id_type=MESH)
        greet() if valid is None else pl.when(valid)(greet)

    if dense:
        load_left = pltpu.make_async_copy(left_hbm, left_v, load_sem.at[0])
        load_right = pltpu.make_async_copy(right_hbm, right_v, load_sem.at[1])
        load_right.start()
        load_left.start()
    source, target = point_features(x_ref[...])
    fown[...] = source.astype(jnp.bfloat16)
    gown[...] = target.astype(jnp.bfloat16)
    for c in range(clusters):
        qbuf[me, c] = q_ref[:, c * size:(c + 1) * size]

    pl.semaphore_wait(
        barrier, sum(1 if valid is None else valid.astype(jnp.int32) for valid, _ in partners)
    )

    sent = []

    def copy_of(block, way, partner):
        return pltpu.make_async_remote_copy(
            src_ref=qbuf.at[block], dst_ref=qbuf.at[block],
            send_sem=send_sem.at[way, block], recv_sem=recv_sem.at[block],
            device_id={"clu": partner}, device_id_type=MESH,
        )

    def send(block, way, partner, valid=None):
        def go():
            copy_of(block, way, partner).start()
        go() if valid is None else pl.when(valid)(go)
        sent.append((block, way, partner, valid))

    def arrive(block, valid=None):
        def go():
            copy_of(block, 0, sib).wait_recv()
        go() if valid is None else pl.when(valid)(go)

    def feature_copy(index):
        off = WINDOW[index]
        return pltpu.make_async_remote_copy(
            src_ref=fown, dst_ref=fbuf.at[index],
            send_sem=fsend_sem.at[index], recv_sem=frecv_sem.at[index],
            device_id={"clu": me + off}, device_id_type=MESH,
        )

    def reaches(off):
        return (me + off >= 0) & (me + off < n)

    for index in (1, 2, 0, 3):
        pl.when(reaches(WINDOW[index]))(lambda index=index: feature_copy(index).start())
    send(me, 3, sib)
    send(me, 2, other_y)
    send(me, 0, me + 4, z < zs - 1)
    send(me, 1, me - 4, z > 0)

    def boundary(k):
        if k <= zs - 1:
            for step, way, partner, more in ((-k, 0, me + 4, z < zs - 1), (k, 1, me - 4, z > 0)):
                there = (z + step >= 0) & (z + step < zs)
                block = block_id(z + step, y, core)
                arrive(block, there)
                send(block, way, partner, there & more)
                send(block, 2, other_y, there)
                send(block, 3, sib, there)
        if k <= zs:
            for step in ((0,) if k == 1 else (-(k - 1), k - 1)):
                there = None if step == 0 else (z + step >= 0) & (z + step < zs)
                block = block_id(z + step, 1 - y, core)
                arrive(block, there)
                send(block, 3, sib, there)
        if k == 1:
            arrive(sib)
        else:
            if k - 1 <= zs - 1:
                for step in (-(k - 1), k - 1):
                    arrive(block_id(z + step, y, 1 - core), (z + step >= 0) & (z + step < zs))
            for step in ((0,) if k == 2 else (-(k - 2), k - 2)):
                there = None if step == 0 else (z + step >= 0) & (z + step < zs)
                arrive(block_id(z + step, 1 - y, 1 - core), there)

    def tile(rows, c):
        squared = jnp.dot(
            rows, gown[:, c * size:(c + 1) * size], preferred_element_type=jnp.float32
        )
        return lax.rsqrt(squared).astype(jnp.bfloat16)

    def set_features(values):
        ft[...] = values.astype(jnp.float32).T.astype(jnp.bfloat16)

    out_ref[...] = jnp.zeros_like(out_ref)

    set_features(fown[...])

    def local_step(step, carry):
        for c in range(clusters):
            e = lax.rem(step + 1 + c, clusters)
            at = pl.ds(pl.multiple_of(e * size, size), size)
            charge = qbuf[me, e] * mask_ref[pl.ds(c, 1), at]
            out_ref[:, c * size:(c + 1) * size] += jnp.dot(
                charge, tile(ft[at, :], c), preferred_element_type=jnp.float32
            )
        return carry

    lax.fori_loop(0, clusters - 1, local_step, 0)

    def near(off):
        there = reaches(off)

        @pl.when(there)
        def _():
            for index, sent_off in enumerate(WINDOW):
                @pl.when(off == -sent_off)
                def _(index=index):
                    feature_copy(index).wait_recv()
                    set_features(fbuf[index])

            def near_step(e, carry):
                at = pl.ds(pl.multiple_of(e * size, size), size)
                charge = qbuf[me + off, e]
                rows = ft[at, :]
                for c in range(clusters):
                    out_ref[:, c * size:(c + 1) * size] += jnp.dot(
                        charge, tile(rows, c), preferred_element_type=jnp.float32
                    )
                return carry

            lax.fori_loop(0, clusters, near_step, 0)

    place = me % 4

    def by_place(values):
        result = values[3]
        for index in (2, 1, 0):
            result = jnp.where(place == index, values[index], result)
        return result

    boundary(1)
    near(by_place((1, -1, 1, -1)))
    boundary(2)
    near(by_place((2, 1, -1, -2)))
    boundary(3)
    near(by_place((-1, 2, -2, 1)))
    boundary(4)
    near(by_place((-2, -2, 2, 2)))
    for k in range(5, zs + 3):
        boundary(k)

    if dense:
        load_right.wait()
        load_left.wait()
        slots_each = req_ref.shape[0] // n
        slots = n * slots_each
        group = size // rank
        row_at = lax.broadcasted_iota(jnp.int32, (columns, size), 1) // rank

        def far_group(g, carry):
            for j in range(group):
                slot = g * group + j
                qgroup[j * columns:(j + 1) * columns, :] = qbuf[slot // slots_each, req_ref[slot]]
            for r in range(clusters):
                picks = [inv_ref[r * slots + g * group + j] for j in range(group)]
                right = jnp.concatenate([right_v[k] for k in picks], axis=0)
                product = lax.dot_general(
                    qgroup[...], right, (((1,), (1,)), ((), ())),
                    preferred_element_type=jnp.float32,
                )
                coefficients = product[:columns]
                for j in range(1, group):
                    coefficients = jnp.where(
                        row_at == j, product[j * columns:(j + 1) * columns], coefficients
                    )
                left = jnp.concatenate([left_v[k] for k in picks], axis=0)
                out_ref[:, r * size:(r + 1) * size] += jnp.dot(
                    coefficients.astype(jnp.bfloat16), left, preferred_element_type=jnp.float32
                )
            return carry

        lax.fori_loop(0, slots // group, far_group, 0)

    for block, way, partner, valid in sent:
        def done(block=block, way=way, partner=partner):
            copy_of(block, way, partner).wait_send()
        done() if valid is None else pl.when(valid)(done)
    for index, off in enumerate(WINDOW):
        pl.when(reaches(off))(lambda index=index: feature_copy(index).wait_send())


def shards(
    charges, coords, requests, near_rows, near_src, local_pairs,
    far_rows, far_slots, far_left, far_right,
):
    columns, width = charges.shape
    pairs, rank, size = far_left.shape
    clusters = width // size
    n = requests.shape[1]
    slots = n * requests.shape[2]
    assert near_rows.shape[1] == clusters * 2 * clusters
    dense = pairs == clusters * slots and slots % (size // rank) == 0

    ids = jnp.arange(clusters, dtype=jnp.int32)
    first = (local_pairs[0, 0][:, None] == ids[None, :])
    second = (local_pairs[0, 1][:, None] == ids[None, :])
    mark = first[:, :, None] & second[:, None, :]
    mark = jnp.any(mark | mark.transpose(0, 2, 1), axis=0)
    mask = jnp.repeat(mark.astype(jnp.bfloat16), size, axis=1)

    code = far_rows[0] * slots + far_slots[0]
    if dense:
        order = jnp.arange(pairs, dtype=jnp.int32)
        inverse = jnp.sum(jnp.where(code[:, None] == order[None, :], order[:, None], 0), axis=0)
    else:
        inverse = code

    any_space = pl.BlockSpec(memory_space=pl.ANY)
    vmem = pl.BlockSpec(memory_space=pltpu.VMEM)
    smem = pl.BlockSpec(memory_space=pltpu.SMEM)
    held = far_left.shape if dense else (1, rank, size)
    half = jnp.bfloat16
    flops = 2 * width * width * 5 * (FEATURES + columns)
    potential = pl.pallas_call(
        functools.partial(body, n, dense),
        out_shape=jax.ShapeDtypeStruct((columns, width), jnp.float32),
        in_specs=[smem, smem, vmem, vmem, vmem, any_space, any_space],
        out_specs=vmem,
        scratch_shapes=[
            pltpu.VMEM((n, clusters, columns, size), half),
            pltpu.VMEM((FEATURES, width), half),
            pltpu.VMEM((4, FEATURES, width), half),
            pltpu.VMEM((width, FEATURES), half),
            pltpu.VMEM((FEATURES, width), half),
            pltpu.VMEM((columns * (size // rank), size), half),
            pltpu.VMEM(held, half),
            pltpu.VMEM(held, half),
            pltpu.SemaphoreType.DMA((4, n)),
            pltpu.SemaphoreType.DMA((n,)),
            pltpu.SemaphoreType.DMA((4,)),
            pltpu.SemaphoreType.DMA((4,)),
            pltpu.SemaphoreType.DMA((2,)),
        ],
        compiler_params=pltpu.CompilerParams(
            collective_id=0, has_side_effects=True, vmem_limit_bytes=56 * 1024 * 1024
        ),
        cost_estimate=pl.CostEstimate(
            flops=flops, bytes_accessed=2 * far_left.size * 2, transcendentals=5 * width * width
        ),
    )(inverse, requests.reshape(-1), charges, coords, mask, far_left, far_right)
    if dense:
        return potential

    blocks = charges.reshape(columns, clusters, size).transpose(1, 0, 2)
    every = lax.all_gather(blocks, "clu", axis=0, tiled=True)
    sources = jnp.arange(slots, dtype=jnp.int32) // requests.shape[2] * clusters
    fetched = every[sources + requests.reshape(-1)]

    def far_step(total, inputs):
        rows_here, slots_here, left_here, right_here = inputs
        coefficients = jnp.einsum(
            "pnb,pkb->pnk", fetched[slots_here], right_here, preferred_element_type=jnp.float32
        ).astype(half)
        term = jnp.einsum(
            "pnk,pka->pna", coefficients, left_here, preferred_element_type=jnp.float32
        )
        return (total.at[rows_here].add(term), None)

    far_inputs = (
        far_rows[0].reshape(-1, 64),
        far_slots[0].reshape(-1, 64),
        far_left.reshape(-1, 64, rank, size),
        far_right.reshape(-1, 64, rank, size),
    )
    total, _ = lax.scan(far_step, jnp.zeros((clusters, columns, size), jnp.float32), far_inputs)
    return potential + total.transpose(1, 0, 2).reshape(columns, width)


def solution(mesh):
    whole = ("groups", "clu")
    in_specs = (
        P(None, whole),
        P(None, whole),
        P(whole, None, None),
        P(whole, None),
        P(whole, None),
        P(whole, None, None),
        P(whole, None),
        P(whole, None),
        P(whole, None, None),
        P(whole, None, None),
    )
    return jax.shard_map(
        shards, mesh=mesh, in_specs=in_specs, out_specs=P(None, whole), check_vma=False
    )
```

time: 347 us -> 89.2 us (0.26)
  waiting for transfers between devices: 128 us -> 0 us
  matrix products: 125 us -> 0 us
  Pallas kernels: 0 us -> 82.5 us
  local copies, waits for them, and re-layouts: 52.8 us -> 4.76 us
  starting transfers between devices: 22.4 us -> 0 us
  between operations: 13.6 us -> 0.02 us
    ppermute x8 -> x0, waiting for transfers between devices: 128 us -> none  [from_behind(): lax.ppermute(value, axis, [(source, source + steps) for source in range(l...]
    dot_general x42 -> x0, matrix products: 125 us -> none  [the longest x16 38.9 us: add_rows(): jnp.einsum('pr,pna->rna', spread(cluster_ids, jnp.float32), values, preci...]
    pallas_call x0 -> x1, Pallas kernels: none -> 82.5 us  [shards(): pl.pallas_call(functools.partial(body, n, dense), out_shape=jax.ShapeDtyp...]
    gather x45 -> x0, local copies, waits for them, and re-layouts: 39.5 us -> none  [the longest x16 15.2 us: near_step(): kernel = kernel_block(coord_blocks[rows_here], window_coord[window_here])]
    ppermute x8 -> x0, starting transfers between devices: 22.4 us -> none  [from_behind(): lax.ppermute(value, axis, [(source, source + steps) for source in range(l...]
    convert_element_type x1, local copies, waits for them, and re-layouts: 6.58 us -> 0.09 us  [shards(): mask = jnp.repeat(mark.astype(jnp.bfloat16), size, axis=1)]
  transfers between devices with their start and end apart: 9 -> 0, of which waited for: 2 -> 0; matrix products, arithmetic and copies ran while one was open for 36% -> 0% of each run, Pallas kernels for 0% -> 0%
where the time goes in v1:
time: 89.2 us; the launch traced here: 88.9 us
  Pallas kernels  82.5 us (92%)
  local copies, waits for them, and re-layouts  4.76 us (5%)
  other arithmetic  1.66 us (2%)
    pallas_call x1, Pallas kernels, shards(): pl.pallas_call(functools.partial(body, n, dense), out_shape=jax.ShapeDtyp...  82.5 us
    unnamed x2, local copies, waits for them, and re-layouts  2.63 us

profile of v1, /device:TPU:19, one launch (start us, length us, event | category | flops | bytes accessed | tf_op | source)
XLA Modules:
  0.0 88.9 jit_solution(2547072915675768745)
XLA Ops:
  0.0 0.7 multiply_add_fusion
  0.7 0.7 select_reduce_fusion.inv_ref
  1.4 0.8 slice_bitcast_fusion.1
  2.2 0.2 or_reduce_fusion
  2.4 0.1 copy.12
  2.5 0.8 copy.11
  3.3 0.6 reshape.63.req_ref
  3.9 0.7 broadcast_in_dim.24
  4.6 82.5 %shard_map.82 = f32[64,2048]{1,0:T(8,128)} custom-call(s32[256]{0:T(256)} %select_reduce_fusion.inv_ref, s32[32]{0:T(128)} %reshape.63.req_ref, bf16[64,2048]{1,0:T(8,128)(2,1)} %q_ref.1, bf16[3,2048]{1,0:T(4,128)(2,1)} %x_ref.1, bf16[8,2048]{1,0:T(8,128)(2,1)} %bitcast.6, bf16[256,32,256]{2,1,0:T(8,128)(2,1)} %left_hbm.1, bf16[256,32,256]{2,1,0:T(8,128)(2,1)} %right_hbm.1), custom_call_target="tpu_custom_call" | custom-call | flops 3355443200 | bytes 8388608 | tf_op jit(solution)/shard_map/pallas_call | solution.py:284
  87.1 1.9 %copy.14 = f32[64,2048]{1,0:T(8,128)} copy(f32[64,2048]{1,0:T(8,128)} %shard_map.82) | data formatting | bytes 1048576
  (2 shorter events, 0.0 us)

commit v2 on v1

--- a/solution.py
+++ b/solution.py
@@ -12,6 +12,7 @@
 MESH = pl.DeviceIdType.MESH
 FEATURES = 16
 WINDOW = (-2, -1, 1, 2)
+PIECES = 1
 
 
 def split3(values):
@@ -81,22 +82,29 @@
 
     sent = []
 
-    def copy_of(block, way, partner):
-        return pltpu.make_async_remote_copy(
-            src_ref=qbuf.at[block], dst_ref=qbuf.at[block],
-            send_sem=send_sem.at[way, block], recv_sem=recv_sem.at[block],
-            device_id={"clu": partner}, device_id_type=MESH,
-        )
+    def copies_of(block, way, partner):
+        each = clusters // PIECES
+        return [
+            pltpu.make_async_remote_copy(
+                src_ref=qbuf.at[block, pl.ds(piece * each, each)],
+                dst_ref=qbuf.at[block, pl.ds(piece * each, each)],
+                send_sem=send_sem.at[way, block, piece], recv_sem=recv_sem.at[block, piece],
+                device_id={"clu": partner}, device_id_type=MESH,
+            )
+            for piece in range(PIECES)
+        ]
 
     def send(block, way, partner, valid=None):
         def go():
-            copy_of(block, way, partner).start()
+            for copy in copies_of(block, way, partner):
+                copy.start()
         go() if valid is None else pl.when(valid)(go)
         sent.append((block, way, partner, valid))
 
     def arrive(block, valid=None):
         def go():
-            copy_of(block, 0, sib).wait_recv()
+            for copy in copies_of(block, 0, sib):
+                copy.wait_recv()
         go() if valid is None else pl.when(valid)(go)
 
     def feature_copy(index):
@@ -142,11 +150,10 @@
                 there = None if step == 0 else (z + step >= 0) & (z + step < zs)
                 arrive(block_id(z + step, 1 - y, 1 - core), there)
 
-    def tile(rows, c):
-        squared = jnp.dot(
-            rows, gown[:, c * size:(c + 1) * size], preferred_element_type=jnp.float32
-        )
-        return lax.rsqrt(squared).astype(jnp.bfloat16)
+    def product(charge, at):
+        squared = jnp.dot(ft[at, :], gown[...], preferred_element_type=jnp.float32)
+        blocks = lax.rsqrt(squared).astype(jnp.bfloat16)
+        return jnp.dot(charge, blocks, preferred_element_type=jnp.float32)
 
     def set_features(values):
         ft[...] = values.astype(jnp.float32).T.astype(jnp.bfloat16)
@@ -155,17 +162,12 @@
 
     set_features(fown[...])
 
-    def local_step(step, carry):
-        for c in range(clusters):
-            e = lax.rem(step + 1 + c, clusters)
-            at = pl.ds(pl.multiple_of(e * size, size), size)
-            charge = qbuf[me, e] * mask_ref[pl.ds(c, 1), at]
-            out_ref[:, c * size:(c + 1) * size] += jnp.dot(
-                charge, tile(ft[at, :], c), preferred_element_type=jnp.float32
-            )
+    def local_step(e, carry):
+        at = pl.ds(pl.multiple_of(e * size, size), size)
+        out_ref[...] += product(qbuf[me, e], at) * mask_ref[pl.ds(e, 1), :]
         return carry
 
-    lax.fori_loop(0, clusters - 1, local_step, 0)
+    lax.fori_loop(0, clusters, local_step, 0)
 
     def near(off):
         there = reaches(off)
@@ -180,12 +182,7 @@
 
             def near_step(e, carry):
                 at = pl.ds(pl.multiple_of(e * size, size), size)
-                charge = qbuf[me + off, e]
-                rows = ft[at, :]
-                for c in range(clusters):
-                    out_ref[:, c * size:(c + 1) * size] += jnp.dot(
-                        charge, tile(rows, c), preferred_element_type=jnp.float32
-                    )
+                out_ref[...] += product(qbuf[me + off, e], at)
                 return carry
 
             lax.fori_loop(0, clusters, near_step, 0)
@@ -243,7 +240,8 @@
 
     for block, way, partner, valid in sent:
         def done(block=block, way=way, partner=partner):
-            copy_of(block, way, partner).wait_send()
+            for copy in copies_of(block, way, partner):
+                copy.wait_send()
         done() if valid is None else pl.when(valid)(done)
     for index, off in enumerate(WINDOW):
         pl.when(reaches(off))(lambda index=index: feature_copy(index).wait_send())
@@ -266,12 +264,12 @@
     second = (local_pairs[0, 1][:, None] == ids[None, :])
     mark = first[:, :, None] & second[:, None, :]
     mark = jnp.any(mark | mark.transpose(0, 2, 1), axis=0)
-    mask = jnp.repeat(mark.astype(jnp.bfloat16), size, axis=1)
+    mask = jnp.repeat(mark.astype(jnp.float32), size, axis=1)
 
     code = far_rows[0] * slots + far_slots[0]
     if dense:
         order = jnp.arange(pairs, dtype=jnp.int32)
-        inverse = jnp.sum(jnp.where(code[:, None] == order[None, :], order[:, None], 0), axis=0)
+        inverse = jnp.max(jnp.where(code[:, None] == order[None, :], order[:, None], 0), axis=0)
     else:
         inverse = code
 
@@ -295,8 +293,8 @@
             pltpu.VMEM((columns * (size // rank), size), half),
             pltpu.VMEM(held, half),
             pltpu.VMEM(held, half),
-            pltpu.SemaphoreType.DMA((4, n)),
-            pltpu.SemaphoreType.DMA((n,)),
+            pltpu.SemaphoreType.DMA((4, n, PIECES)),
+            pltpu.SemaphoreType.DMA((n, PIECES)),
             pltpu.SemaphoreType.DMA((4,)),
             pltpu.SemaphoreType.DMA((4,)),
             pltpu.SemaphoreType.DMA((2,)),

time: 89.2 us -> 57.4 us (0.64)
  Pallas kernels: 82.5 us -> 50.6 us
    pallas_call x1, Pallas kernels: 82.5 us -> 50.6 us  [shards(): pl.pallas_call(functools.partial(body, n, dense), out_shape=jax.ShapeDtyp...]
where the time goes in v2:
time: 57.4 us; the launch traced here: 57 us
  Pallas kernels  50.6 us (88%)
  local copies, waits for them, and re-layouts  4.76 us (8%)
  other arithmetic  1.66 us (3%)
    pallas_call x1, Pallas kernels, shards(): pl.pallas_call(functools.partial(body, n, dense), out_shape=jax.ShapeDtyp...  50.6 us
    unnamed x2, local copies, waits for them, and re-layouts  2.63 us

profile of v2, /device:TPU:19, one launch (start us, length us, event | category | flops | bytes accessed | tf_op | source)
XLA Modules:
  0.0 57.0 jit_solution(3868066768075567653)
XLA Ops:
  0.0 0.7 %multiply_add_fusion = s32[1,256]{1,0:T(1,128)S(1)} fusion(s32[1,256]{1,0:T(1,128)} %param.15, s32[1,256]{1,0:T(1,128)} %param.14), kind=kLoop, calls=%fused_computation.5 | loop fusion | flops 512 | bytes 3072 | tf_op jit(solution)/shard_map/add | solution.py:269
  0.7 0.7 %select_reduce_fusion.inv_ref = s32[256]{0:T(256)} fusion(s32[256]{0:T(256)S(1)} %bitcast.7), kind=kLoop, calls=%fused_computation | loop fusion | flops 196352 | bytes 2048 | tf_op jit(solution)/shard_map/reduce_max | solution.py:272
  1.4 0.8 %slice_bitcast_fusion.1 = (s32[16]{0:T(128)S(1)}, s32[16]{0:T(128)S(1)}) fusion(s32[1,2,16]{2,1,0:T(2,128)} %param.13), kind=kLoop, calls=%fused_computation.7 | loop fusion | bytes 256 | tf_op jit(solution)/shard_map/eq | solution.py:263
  2.2 0.2 or_reduce_fusion
  2.4 0.1 copy.12
  2.5 0.8 %copy.11 = s32[1,16,2]{2,1,0:T(8,128)S(1)} copy(s32[1,16,2]{1,2,0:T(2,128)} %param.12) | data formatting | bytes 256 | tf_op args[2]
  3.3 0.6 %reshape.63.req_ref = s32[32]{0:T(128)} reshape(s32[1,16,2]{2,1,0:T(8,128)S(1)} %copy.11) | data formatting | bytes 256 | tf_op jit(solution)/shard_map/reshape | solution.py:308
  3.8 0.7 %broadcast_in_dim.24 = f32[8,8,256]{2,0,1:T(8,128)} broadcast(f32[8,8]{0,1:T(8,128)S(1)} %copy.12), dimensions={0,1} | broadcast | bytes 65792 | tf_op jit(solution)/shard_map/broadcast_in_dim | solution.py:267
  4.6 50.6 %shard_map.82 = f32[64,2048]{1,0:T(8,128)} custom-call(s32[256]{0:T(256)} %select_reduce_fusion.inv_ref, s32[32]{0:T(128)} %reshape.63.req_ref, bf16[64,2048]{1,0:T(8,128)(2,1)} %q_ref.1, bf16[3,2048]{1,0:T(4,128)(2,1)} %x_ref.1, f32[8,2048]{1,0:T(8,128)} %bitcast.6, bf16[256,32,256]{2,1,0:T(8,128)(2,1)} %left_hbm.1, bf16[256,32,256]{2,1,0:T(8,128)(2,1)} %right_hbm.1), custom_call_target="tpu_custom_call" | custom-call | flops 3355443200 | bytes 8388608 | tf_op jit(solution)/shard_map/pallas_call | solution.py:282
  55.1 1.9 %copy.14 = f32[64,2048]{1,0:T(8,128)} copy(f32[64,2048]{1,0:T(8,128)} %shard_map.82) | data formatting | bytes 1048576
  (2 shorter events, 0.0 us)

commit v3 on v2

--- a/solution.py
+++ b/solution.py
@@ -13,6 +13,7 @@
 FEATURES = 16
 WINDOW = (-2, -1, 1, 2)
 PIECES = 1
+TOGETHER = 4
 
 
 def split3(values):
@@ -37,9 +38,9 @@
 
 def body(
     n, dense,
-    inv_ref, req_ref, q_ref, x_ref, mask_ref, left_hbm, right_hbm,
+    req_ref, pairs_ref, rows_ref, slots_ref, q_ref, x_ref, left_hbm, right_hbm,
     out_ref,
-    qbuf, fown, fbuf, ft, gown, qgroup, left_v, right_v,
+    qbuf, fown, fbuf, ft, gown, mask_ref, left_v, right_v, inv_v, inv_ref,
     send_sem, recv_sem, fsend_sem, frecv_sem, load_sem,
 ):
     columns, width = q_ref.shape
@@ -70,9 +71,6 @@
         load_right = pltpu.make_async_copy(right_hbm, right_v, load_sem.at[1])
         load_right.start()
         load_left.start()
-    source, target = point_features(x_ref[...])
-    fown[...] = source.astype(jnp.bfloat16)
-    gown[...] = target.astype(jnp.bfloat16)
     for c in range(clusters):
         qbuf[me, c] = q_ref[:, c * size:(c + 1) * size]
 
@@ -118,41 +116,48 @@
     def reaches(off):
         return (me + off >= 0) & (me + off < n)
 
+    send(me, 0, me + 4, z < zs - 1)
+    send(me, 1, me - 4, z > 0)
+    send(me, 2, other_y)
+    send(me, 3, sib)
+    source, target = point_features(x_ref[...])
+    fown[...] = source.astype(jnp.bfloat16)
+    gown[...] = target.astype(jnp.bfloat16)
     for index in (1, 2, 0, 3):
         pl.when(reaches(WINDOW[index]))(lambda index=index: feature_copy(index).start())
-    send(me, 3, sib)
-    send(me, 2, other_y)
-    send(me, 0, me + 4, z < zs - 1)
-    send(me, 1, me - 4, z > 0)
-
-    def boundary(k):
-        if k <= zs - 1:
+
+    def on_z(step):
+        return None if step == 0 else (z + step >= 0) & (z + step < zs)
+
+    def both_ways(k):
+        return (0,) if k == 0 else (-k, k)
+
+    def along_z(k):
+        if 1 <= k < zs:
             for step, way, partner, more in ((-k, 0, me + 4, z < zs - 1), (k, 1, me - 4, z > 0)):
-                there = (z + step >= 0) & (z + step < zs)
                 block = block_id(z + step, y, core)
-                arrive(block, there)
-                send(block, way, partner, there & more)
-                send(block, 2, other_y, there)
-                send(block, 3, sib, there)
-        if k <= zs:
-            for step in ((0,) if k == 1 else (-(k - 1), k - 1)):
-                there = None if step == 0 else (z + step >= 0) & (z + step < zs)
+                arrive(block, on_z(step))
+                send(block, way, partner, on_z(step) & more)
+                send(block, 2, other_y, on_z(step))
+                send(block, 3, sib, on_z(step))
+
+    def across_y(k):
+        if 0 <= k < zs:
+            for step in both_ways(k):
                 block = block_id(z + step, 1 - y, core)
-                arrive(block, there)
-                send(block, 3, sib, there)
-        if k == 1:
-            arrive(sib)
-        else:
-            if k - 1 <= zs - 1:
-                for step in (-(k - 1), k - 1):
-                    arrive(block_id(z + step, y, 1 - core), (z + step >= 0) & (z + step < zs))
-            for step in ((0,) if k == 2 else (-(k - 2), k - 2)):
-                there = None if step == 0 else (z + step >= 0) & (z + step < zs)
-                arrive(block_id(z + step, 1 - y, 1 - core), there)
-
-    def product(charge, at):
+                arrive(block, on_z(step))
+                send(block, 3, sib, on_z(step))
+
+    def from_sibling(k, y_at):
+        if 0 <= k < zs:
+            for step in both_ways(k):
+                arrive(block_id(z + step, y_at, 1 - core), on_z(step))
+
+    def product(block, first, count):
+        at = pl.ds(pl.multiple_of(first * size, size), count * size)
         squared = jnp.dot(ft[at, :], gown[...], preferred_element_type=jnp.float32)
         blocks = lax.rsqrt(squared).astype(jnp.bfloat16)
+        charge = jnp.concatenate([qbuf[block, first + i] for i in range(count)], axis=1)
         return jnp.dot(charge, blocks, preferred_element_type=jnp.float32)
 
     def set_features(values):
@@ -161,13 +166,30 @@
     out_ref[...] = jnp.zeros_like(out_ref)
 
     set_features(fown[...])
+    entry = lax.broadcasted_iota(jnp.int32, (clusters, width), 0) * clusters
+    entry = entry + lax.broadcasted_iota(jnp.int32, (clusters, width), 1) // size
+    mark = entry < 0
+    for k in range(pairs_ref.shape[2]):
+        first, second = pairs_ref[0, 0, k], pairs_ref[0, 1, k]
+        mark = mark | (entry == first * clusters + second) | (entry == second * clusters + first)
+    mask_ref[...] = mark.astype(jnp.float32)
+
+    if dense:
+        slots = n * req_ref.shape[2]
+        pairs = clusters * slots
+        code = jnp.broadcast_to(rows_ref[...] * slots + slots_ref[...], (8, pairs)).T[:, :1]
+        found = code == lax.broadcasted_iota(jnp.int32, (pairs, pairs), 1)
+        number = lax.broadcasted_iota(jnp.int32, (pairs, pairs), 0)
+        table = jnp.max(jnp.where(found, number, 0), axis=0, keepdims=True)
+        inv_v[...] = jnp.broadcast_to(table, (8, pairs))
+        to_scalars = pltpu.make_async_copy(inv_v, inv_ref, load_sem.at[2])
+        to_scalars.start()
 
     def local_step(e, carry):
-        at = pl.ds(pl.multiple_of(e * size, size), size)
-        out_ref[...] += product(qbuf[me, e], at) * mask_ref[pl.ds(e, 1), :]
+        out_ref[...] += product(me, e, 1) * mask_ref[pl.ds(e, 1), :]
         return carry
 
-    lax.fori_loop(0, clusters, local_step, 0)
+    lax.fori_loop(0, clusters, local_step, 0, unroll=2)
 
     def near(off):
         there = reaches(off)
@@ -180,12 +202,11 @@
                     feature_copy(index).wait_recv()
                     set_features(fbuf[index])
 
-            def near_step(e, carry):
-                at = pl.ds(pl.multiple_of(e * size, size), size)
-                out_ref[...] += product(qbuf[me + off, e], at)
+            def near_step(step, carry):
+                out_ref[...] += product(me + off, step * TOGETHER, TOGETHER)
                 return carry
 
-            lax.fori_loop(0, clusters, near_step, 0)
+            lax.fori_loop(0, clusters // TOGETHER, near_step, 0)
 
     place = me % 4
 
@@ -195,44 +216,58 @@
             result = jnp.where(place == index, values[index], result)
         return result
 
-    boundary(1)
+    along_z(1)
+    from_sibling(0, y)
     near(by_place((1, -1, 1, -1)))
-    boundary(2)
+    along_z(2)
+    across_y(0)
+    from_sibling(1, y)
+    from_sibling(0, 1 - y)
     near(by_place((2, 1, -1, -2)))
-    boundary(3)
+    along_z(3)
+    across_y(1)
+    from_sibling(2, y)
+    from_sibling(1, 1 - y)
     near(by_place((-1, 2, -2, 1)))
-    boundary(4)
+    across_y(2)
+    from_sibling(3, y)
     near(by_place((-2, -2, 2, 2)))
-    for k in range(5, zs + 3):
-        boundary(k)
+    across_y(3)
+    from_sibling(2, 1 - y)
+    from_sibling(3, 1 - y)
+    for k in range(4, zs):
+        along_z(k)
+        across_y(k)
+        from_sibling(k, y)
+        from_sibling(k, 1 - y)
 
     if dense:
         load_right.wait()
         load_left.wait()
-        slots_each = req_ref.shape[0] // n
-        slots = n * slots_each
+        to_scalars.wait()
+        slots_each = req_ref.shape[2]
         group = size // rank
-        row_at = lax.broadcasted_iota(jnp.int32, (columns, size), 1) // rank
 
         def far_group(g, carry):
+            def pick(r, j):
+                return inv_ref[0, r * slots + g * group + j]
+
+            parts = []
             for j in range(group):
                 slot = g * group + j
-                qgroup[j * columns:(j + 1) * columns, :] = qbuf[slot // slots_each, req_ref[slot]]
+                owner = slot // slots_each
+                charge = qbuf[owner, req_ref[0, owner, slot % slots_each]]
+                right = jnp.concatenate([right_v[pick(r, j)] for r in range(clusters)], axis=0)
+                parts.append(lax.dot_general(
+                    right, charge, (((1,), (1,)), ((), ())), preferred_element_type=jnp.float32
+                ))
             for r in range(clusters):
-                picks = [inv_ref[r * slots + g * group + j] for j in range(group)]
-                right = jnp.concatenate([right_v[k] for k in picks], axis=0)
-                product = lax.dot_general(
-                    qgroup[...], right, (((1,), (1,)), ((), ())),
-                    preferred_element_type=jnp.float32,
+                turned = jnp.concatenate(
+                    [part[r * rank:(r + 1) * rank] for part in parts], axis=0
                 )
-                coefficients = product[:columns]
-                for j in range(1, group):
-                    coefficients = jnp.where(
-                        row_at == j, product[j * columns:(j + 1) * columns], coefficients
-                    )
-                left = jnp.concatenate([left_v[k] for k in picks], axis=0)
+                left = jnp.concatenate([left_v[pick(r, j)] for j in range(group)], axis=0)
                 out_ref[:, r * size:(r + 1) * size] += jnp.dot(
-                    coefficients.astype(jnp.bfloat16), left, preferred_element_type=jnp.float32
+                    turned.T.astype(jnp.bfloat16), left, preferred_element_type=jnp.float32
                 )
             return carry
 
@@ -259,20 +294,6 @@
     assert near_rows.shape[1] == clusters * 2 * clusters
     dense = pairs == clusters * slots and slots % (size // rank) == 0
 
-    ids = jnp.arange(clusters, dtype=jnp.int32)
-    first = (local_pairs[0, 0][:, None] == ids[None, :])
-    second = (local_pairs[0, 1][:, None] == ids[None, :])
-    mark = first[:, :, None] & second[:, None, :]
-    mark = jnp.any(mark | mark.transpose(0, 2, 1), axis=0)
-    mask = jnp.repeat(mark.astype(jnp.float32), size, axis=1)
-
-    code = far_rows[0] * slots + far_slots[0]
-    if dense:
-        order = jnp.arange(pairs, dtype=jnp.int32)
-        inverse = jnp.max(jnp.where(code[:, None] == order[None, :], order[:, None], 0), axis=0)
-    else:
-        inverse = code
-
     any_space = pl.BlockSpec(memory_space=pl.ANY)
     vmem = pl.BlockSpec(memory_space=pltpu.VMEM)
     smem = pl.BlockSpec(memory_space=pltpu.SMEM)
@@ -282,7 +303,7 @@
     potential = pl.pallas_call(
         functools.partial(body, n, dense),
         out_shape=jax.ShapeDtypeStruct((columns, width), jnp.float32),
-        in_specs=[smem, smem, vmem, vmem, vmem, any_space, any_space],
+        in_specs=[smem, smem, vmem, vmem, vmem, vmem, any_space, any_space],
         out_specs=vmem,
         scratch_shapes=[
             pltpu.VMEM((n, clusters, columns, size), half),
@@ -290,14 +311,16 @@
             pltpu.VMEM((4, FEATURES, width), half),
             pltpu.VMEM((width, FEATURES), half),
             pltpu.VMEM((FEATURES, width), half),
-            pltpu.VMEM((columns * (size // rank), size), half),
+            pltpu.VMEM((clusters, width), jnp.float32),
             pltpu.VMEM(held, half),
             pltpu.VMEM(held, half),
+            pltpu.VMEM((8, pairs), jnp.int32),
+            pltpu.SMEM((8, pairs), jnp.int32),
             pltpu.SemaphoreType.DMA((4, n, PIECES)),
             pltpu.SemaphoreType.DMA((n, PIECES)),
             pltpu.SemaphoreType.DMA((4,)),
             pltpu.SemaphoreType.DMA((4,)),
-            pltpu.SemaphoreType.DMA((2,)),
+            pltpu.SemaphoreType.DMA((3,)),
         ],
         compiler_params=pltpu.CompilerParams(
             collective_id=0, has_side_effects=True, vmem_limit_bytes=56 * 1024 * 1024
@@ -305,7 +328,7 @@
         cost_estimate=pl.CostEstimate(
             flops=flops, bytes_accessed=2 * far_left.size * 2, transcendentals=5 * width * width
         ),
-    )(inverse, requests.reshape(-1), charges, coords, mask, far_left, far_right)
+    )(requests, local_pairs, far_rows, far_slots, charges, coords, far_left, far_right)
     if dense:
         return potential
 

time: 57.4 us -> 45.1 us (0.79)
  Pallas kernels: 50.6 us -> 41.6 us
  other arithmetic: 1.66 us -> 0 us
  local copies, waits for them, and re-layouts: 4.76 us -> 3.22 us
    pallas_call x1, Pallas kernels: 50.6 us -> 41.6 us  [shards(): pl.pallas_call(functools.partial(body, n, dense), out_shape=jax.ShapeDtyp...]
    eq x1 -> x0, local copies, waits for them, and re-layouts: 0.76 us -> none  [shards(): first = local_pairs[0, 0][:, None] == ids[None, :]]
    reduce_max x1 -> x0, other arithmetic: 0.71 us -> none  [shards(): jnp.max(jnp.where(code[:, None] == order[None, :], order[:, None], 0), ax...]
    add x1 -> x0, other arithmetic: 0.71 us -> none  [shards(): code = far_rows[0] * slots + far_slots[0]]
    broadcast_in_dim x1 -> x0, local copies, waits for them, and re-layouts: 0.7 us -> none  [shards(): mask = jnp.repeat(mark.astype(jnp.float32), size, axis=1)]
    reshape x1 -> x0, local copies, waits for them, and re-layouts: 0.59 us -> none  [shards(): requests.reshape(-1)]
    unnamed x2, local copies, waits for them, and re-layouts: 2.63 us -> 3.22 us
where the time goes in v3:
time: 45.1 us; the launch traced here: 44.9 us
  Pallas kernels  41.6 us (92%)
  local copies, waits for them, and re-layouts  3.22 us (7%)
    pallas_call x1, Pallas kernels, shards(): pl.pallas_call(functools.partial(body, n, dense), out_shape=jax.ShapeDtyp...  41.6 us
    unnamed x2, local copies, waits for them, and re-layouts  3.22 us

profile of v3, /device:TPU:19, one launch (start us, length us, event | category | flops | bytes accessed | tf_op | source)
XLA Modules:
  0.0 44.9 jit_solution(9282142769829680331)
XLA Ops:
  0.0 1.4 %copy.9.req_ref = s32[1,16,2]{2,1,0:T(8,128)} copy(s32[1,16,2]{1,2,0:T(2,128)} %param.12) | data formatting | bytes 256 | tf_op args[2]
  1.4 41.6 %shard_map.82 = f32[64,2048]{1,0:T(8,128)} custom-call(s32[1,16,2]{2,1,0:T(8,128)} %copy.9.req_ref, s32[1,2,16]{2,1,0:T(2,128)} %pairs_ref.1, s32[1,256]{1,0:T(1,128)} %rows_ref.1, s32[1,256]{1,0:T(1,128)} %slots_ref.1, bf16[64,2048]{1,0:T(8,128)(2,1)} %q_ref.1, bf16[3,2048]{1,0:T(4,128)(2,1)} %x_ref.1, bf16[256,32,256]{2,1,0:T(8,128)(2,1)} %left_hbm.1, ...), custom_call_target="tpu_custom_call" | custom-call | flops 3355443200 | bytes 8388608 | tf_op jit(solution)/shard_map/pallas_call | solution.py:303
  43.0 1.9 %copy.11 = f32[64,2048]{1,0:T(8,128)} copy(f32[64,2048]{1,0:T(8,128)} %shard_map.82) | data formatting | bytes 1048576

commit v4 on v3

--- a/solution.py
+++ b/solution.py
@@ -191,10 +191,8 @@
 
     lax.fori_loop(0, clusters, local_step, 0, unroll=2)
 
-    def near(off):
-        there = reaches(off)
-
-        @pl.when(there)
+    def near_start(off):
+        @pl.when(reaches(off))
         def _():
             for index, sent_off in enumerate(WINDOW):
                 @pl.when(off == -sent_off)
@@ -202,11 +200,14 @@
                     feature_copy(index).wait_recv()
                     set_features(fbuf[index])
 
+    def near_part(off, first, last):
+        @pl.when(reaches(off))
+        def _():
             def near_step(step, carry):
                 out_ref[...] += product(me + off, step * TOGETHER, TOGETHER)
                 return carry
 
-            lax.fori_loop(0, clusters // TOGETHER, near_step, 0)
+            lax.fori_loop(first, last, near_step, 0)
 
     place = me % 4
 
@@ -216,32 +217,47 @@
             result = jnp.where(place == index, values[index], result)
         return result
 
+    steps = clusters // TOGETHER
     along_z(1)
     from_sibling(0, y)
-    near(by_place((1, -1, 1, -1)))
+    off = by_place((1, -1, 1, -1))
+    near_start(off)
+    near_part(off, 0, steps // 2)
     along_z(2)
     across_y(0)
+    near_part(off, steps // 2, steps)
     from_sibling(1, y)
     from_sibling(0, 1 - y)
-    near(by_place((2, 1, -1, -2)))
+    off = by_place((2, 1, -1, -2))
+    near_start(off)
+    near_part(off, 0, steps // 2)
     along_z(3)
     across_y(1)
+    near_part(off, steps // 2, steps)
     from_sibling(2, y)
     from_sibling(1, 1 - y)
-    near(by_place((-1, 2, -2, 1)))
+    off = by_place((-1, 2, -2, 1))
+    near_start(off)
+    near_part(off, 0, steps)
     across_y(2)
     from_sibling(3, y)
-    near(by_place((-2, -2, 2, 2)))
-    across_y(3)
+    off = by_place((-2, -2, 2, 2))
+    near_start(off)
+    near_part(off, 0, steps)
     from_sibling(2, 1 - y)
-    from_sibling(3, 1 - y)
-    for k in range(4, zs):
-        along_z(k)
-        across_y(k)
-        from_sibling(k, y)
-        from_sibling(k, 1 - y)
-
-    if dense:
+
+    def last_arrivals():
+        across_y(3)
+        from_sibling(3, 1 - y)
+        for k in range(4, zs):
+            along_z(k)
+            across_y(k)
+            from_sibling(k, y)
+            from_sibling(k, 1 - y)
+
+    if not dense:
+        last_arrivals()
+    else:
         load_right.wait()
         load_left.wait()
         to_scalars.wait()
@@ -256,7 +272,10 @@
             for j in range(group):
                 slot = g * group + j
                 owner = slot // slots_each
-                charge = qbuf[owner, req_ref[0, owner, slot % slots_each]]
+                wanted = req_ref[0, owner, slot % slots_each]
+                charge = qbuf[owner, 0]
+                for c in range(1, clusters):
+                    charge = jnp.where(wanted == c, qbuf[owner, c], charge)
                 right = jnp.concatenate([right_v[pick(r, j)] for r in range(clusters)], axis=0)
                 parts.append(lax.dot_general(
                     right, charge, (((1,), (1,)), ((), ())), preferred_element_type=jnp.float32
@@ -271,7 +290,10 @@
                 )
             return carry
 
-        lax.fori_loop(0, slots // group, far_group, 0)
+        above = (2 * z < zs).astype(jnp.int32)
+        lax.fori_loop(1 - above, zs - above, far_group, 0)
+        last_arrivals()
+        far_group(above * (zs - 1), 0)
 
     for block, way, partner, valid in sent:
         def done(block=block, way=way, partner=partner):
@@ -292,7 +314,7 @@
     n = requests.shape[1]
     slots = n * requests.shape[2]
     assert near_rows.shape[1] == clusters * 2 * clusters
-    dense = pairs == clusters * slots and slots % (size // rank) == 0
+    dense = pairs == clusters * slots and size // rank == 4 * requests.shape[2] and n <= 16
 
     any_space = pl.BlockSpec(memory_space=pl.ANY)
     vmem = pl.BlockSpec(memory_space=pltpu.VMEM)

time: 45.1 us -> 45.4 us (level)
  no operation moved by 1% of the time
where the time goes in v4:
time: 45.4 us; the launch traced here: 45 us
  Pallas kernels  41.7 us (92%)
  local copies, waits for them, and re-layouts  3.22 us (7%)
    pallas_call x1, Pallas kernels, shards(): pl.pallas_call(functools.partial(body, n, dense), out_shape=jax.ShapeDtyp...  41.7 us
    unnamed x2, local copies, waits for them, and re-layouts  3.22 us

profile of v4, /device:TPU:19, one launch (start us, length us, event | category | flops | bytes accessed | tf_op | source)
XLA Modules:
  0.0 45.0 jit_solution(15604606694069112876)
XLA Ops:
  0.0 1.4 %copy.9.req_ref = s32[1,16,2]{2,1,0:T(8,128)} copy(s32[1,16,2]{1,2,0:T(2,128)} %param.12) | data formatting | bytes 256 | tf_op args[2]
  1.4 41.7 %shard_map.82 = f32[64,2048]{1,0:T(8,128)} custom-call(s32[1,16,2]{2,1,0:T(8,128)} %copy.9.req_ref, s32[1,2,16]{2,1,0:T(2,128)} %pairs_ref.1, s32[1,256]{1,0:T(1,128)} %rows_ref.1, s32[1,256]{1,0:T(1,128)} %slots_ref.1, bf16[64,2048]{1,0:T(8,128)(2,1)} %q_ref.1, bf16[3,2048]{1,0:T(4,128)(2,1)} %x_ref.1, bf16[256,32,256]{2,1,0:T(8,128)(2,1)} %left_hbm.1, ...), custom_call_target="tpu_custom_call" | custom-call | flops 3355443200 | bytes 8388608 | tf_op jit(solution)/shard_map/pallas_call | solution.py:325
  43.1 1.9 %copy.11 = f32[64,2048]{1,0:T(8,128)} copy(f32[64,2048]{1,0:T(8,128)} %shard_map.82) | data formatting | bytes 1048576
